TPU v7x, 256 devices: a whole 4x4x8 slice. The times are simulated.
256 devices in a mesh: parent: 4 (over x_lo, core), child: 4 (over y), tile: 16 (over z, x_hi).
Axes of the slice: x: 4 (x_hi: 2, x_lo: 2; x = x_hi * 2 + x_lo), y: 4, z: 8, core: 2. Of those that a mesh axis runs over, the one named last changes fastest.
Arguments:
- children: float32 [16, 4, 512, 2048], P(('parent', 'child'), None, 'tile'), parts along dimension 0, as said below
Outputs:
- parent_map: float32 [16, 2, 512, 4, 1024], P('parent', None, 'tile', 'child'), parts along dimension 0
There are 4 independent parts, one for each index of `parent`. A program takes and returns all parts, laid end to end along the dimension named above; each array names one. Nothing has to cross between parts.
Inputs may be any that keep to these rules, and one draw needn't show every extreme that they name: `children`: each child's map, read as a matrix of order 4 * 512 in edge-major order, is exactly symmetric and has smallest eigenvalue 0.2 or more.
All inputs are finite; a program needn't handle non-finite values.
Results may differ from a plain program's by a relative error of at most 0.000088.
Values sent between devices are 32-bit elements; how exact they have to be, the bound alone decides.
No kernel may reach another device: no remote copies, remote signals or barrier semaphores. Data moves between devices by JAX's collectives and lax.ppermute only.
A program may use at most 128 MiB of HBM per device.

v0:
```python
import jax
import jax.numpy as jnp
from jax import lax
from jax.experimental import pallas as pl
from jax.experimental.pallas import tpu as pltpu
from jax.sharding import PartitionSpec as P

precise = lax.Precision.HIGHEST
BLOCK = 128
GROUP = 8


def product_high(left_mat, right_mat):
    return jnp.dot(left_mat, right_mat, precision=precise, preferred_element_type=jnp.float32)


def product_left_t(left_mat, right_mat, precision=lax.Precision.HIGH):
    return lax.dot_general(
        left_mat,
        right_mat,
        (((0,), (0,)), ((), ())),
        precision=precision,
        preferred_element_type=jnp.float32,
    )


def split(mat):
    high = mat.astype(jnp.bfloat16)
    return high, (mat - high.astype(jnp.float32)).astype(jnp.bfloat16)


def wide_left(mat):
    high, low = split(mat)
    return jnp.concatenate([high, low, high], axis=1)


def wide_right(mat):
    high, low = split(mat)
    return jnp.concatenate([high, high, low], axis=0)


def product_wide(left_wide, right_wide):
    return jnp.dot(left_wide, right_wide, preferred_element_type=jnp.float32)


def pivot_group(rows, g):
    shape = (GROUP, BLOCK)
    sub = lax.broadcasted_iota(jnp.int32, shape, 0)
    lane = lax.broadcasted_iota(jnp.int32, shape, 1)
    first = GROUP * g

    def row_of(v, j):
        return jnp.broadcast_to(v[j : j + 1, :], shape)

    def col_of(v, j):
        return jnp.broadcast_to(v[:, first + j : first + j + 1], shape)

    top = rows[g]
    cols = [col_of(top, j) for j in range(GROUP)]
    pivot = row_of(cols[0], 0)
    for j in range(GROUP):
        inverse = 1.0 / pivot
        if j + 1 < GROUP:
            ahead = cols[j] * row_of(cols[j + 1], j)
            pivot = row_of(cols[j + 1], j + 1) - row_of(ahead, j + 1) * inverse
        scaled = jnp.where(lane == first + j, inverse, row_of(top, j) * inverse)
        cleared = jnp.where(lane == first + j, 0.0, top)
        top = jnp.where(sub == j, scaled, cleared - cols[j] * scaled)
        for l in range(j + 1, GROUP):
            entry = row_of(cols[l], j)
            cols[l] = jnp.where(sub == j, entry * inverse, cols[l] - (cols[j] * entry) * inverse)
    spread = [row_of(top, j) for j in range(GROUP)]
    out = []
    for h, v in enumerate(rows):
        if h == g:
            out.append(top)
            continue
        terms = [col_of(v, j) * spread[j] for j in range(GROUP)]
        while len(terms) > 1:
            terms = [terms[i] + terms[i + 1] for i in range(0, len(terms), 2)]
        pivots = (lane >= first) & (lane < first + GROUP)
        out.append(jnp.where(pivots, 0.0, v) - terms[0])
    return out


def invert_blocks(mats, width, beside=None):
    count = BLOCK // GROUP
    inner = width // GROUP

    def body(p, carry):
        if beside is not None:
            beside(p)
        out = []
        for i in range(len(mats)):
            groups = list(carry[count * i : count * (i + 1)])
            panel = groups[:inner]
            for g in range(inner):
                panel = pivot_group(panel, g)
            panel = jnp.concatenate(panel, axis=0)
            rest = jnp.concatenate(groups[inner:], axis=0)
            update = product_high(rest[:, :width], panel)
            lanes = lax.broadcasted_iota(jnp.int32, rest.shape, 1)
            rest = jnp.where(lanes < width, 0.0, rest) - update
            turned = pltpu.roll(jnp.concatenate([rest, panel], axis=0), BLOCK - width, 1)
            out += [turned[GROUP * h : GROUP * (h + 1)] for h in range(count)]
        return tuple(out)

    init = tuple(m[GROUP * h : GROUP * (h + 1), :] for m in mats for h in range(count))
    res = lax.fori_loop(0, BLOCK // width, body, init)
    return [jnp.concatenate(res[count * i : count * (i + 1)], axis=0) for i in range(len(mats))]


def even_kernel(half_ref, mine_ref, other_ref, inv_ref):
    n = inv_ref.shape[0]
    h = n // 2
    mine = pl.ds(pl.multiple_of(half_ref[0] * h, h), h)
    other = pl.ds(pl.multiple_of((1 - half_ref[0]) * h, h), h)
    inv_ref[:, mine] = mine_ref[...]
    inv_ref[:, other] = other_ref[...]
    for k in range(n // BLOCK):
        ks = slice(k * BLOCK, (k + 1) * BLOCK)
        (diag,) = invert_blocks([inv_ref[ks, ks]], 64)
        inv_ref[ks, ks] = jnp.eye(BLOCK, dtype=jnp.float32)
        row = product_high(diag, inv_ref[ks, :])
        for m in range(n // BLOCK):
            if m != k:
                ms = slice(m * BLOCK, (m + 1) * BLOCK)
                col = inv_ref[ms, ks]
                inv_ref[ms, ks] = jnp.zeros((BLOCK, BLOCK), jnp.float32)
                inv_ref[ms, :] = inv_ref[ms, :] - product_high(col, row)
        inv_ref[ks, :] = row


def even_inverse(half, mine, other):
    n = mine.shape[0]
    return pl.pallas_call(
        even_kernel,
        out_shape=jax.ShapeDtypeStruct((n, n), jnp.float32),
        in_specs=[pl.BlockSpec(memory_space=pltpu.SMEM)]
        + [pl.BlockSpec(memory_space=pltpu.VMEM)] * 2,
        out_specs=pl.BlockSpec(memory_space=pltpu.VMEM),
        compiler_params=pltpu.CompilerParams(vmem_limit_bytes=40 * 1024 * 1024),
        cost_estimate=pl.CostEstimate(flops=10**10, bytes_accessed=10**8, transcendentals=0),
        name="even_inverse",
    )(half, mine, other)


def middle_kernel(
    inv_own, inv_far, c0, c1, c2, c3, b, k_own, corner, across, corner_far, near, away, w0, w1, w2, w3
):
    n = corner.shape[0]
    slab = b.shape[1]

    def chunk(m):
        return pl.ds(pl.multiple_of(m * BLOCK, BLOCK), BLOCK)

    for i, (inv, c, wide) in enumerate(
        ((inv_own, c0, w0), (inv_own, c1, w1), (inv_far, c3, w3), (inv_far, c2, w2))
    ):

        def solved(m, carry, i=i, inv=inv, c=c, wide=wide):
            rows = product_high(inv[chunk(m), :], c[...])
            if i < 2:
                k_own[chunk(m), i * n : (i + 1) * n] = rows
            high, low = split(rows)
            wide[0, chunk(m), :] = high
            wide[1, chunk(m), :] = high
            wide[2, chunk(m), :] = low
            return carry

        lax.fori_loop(0, n // BLOCK, solved, 0)
    r0, r1, r2, r3 = (w[...].reshape(3 * n, n) for w in (w0, w1, w2, w3))

    def schur(m, carry):
        l0, l1, l2, l3 = (wide_left(c[:, chunk(m)].T) for c in (c0, c1, c2, c3))
        corner[chunk(m), :] = product_wide(l0, r0) + product_wide(l3, r3)
        across[chunk(m), :] = product_wide(l0, r1) + product_wide(l3, r2)
        corner_far[chunk(m), :] = product_wide(l1, r1) + product_wide(l2, r2)
        return carry

    lax.fori_loop(0, n // BLOCK, schur, 0)
    own = wide_left(jnp.concatenate([b[0, :, :n], b[1, :, :n]], axis=0))
    far = wide_left(jnp.concatenate([b[2, :, :n], b[3, :, :n]], axis=0))
    half = 2 * slab
    near[:half, :] = -product_wide(own, r0)
    near[half:, :] = -product_wide(far, r3)
    away[:half, :] = -product_wide(own, r1)
    away[half:, :] = -product_wide(far, r2)
    for ref, siblings_of in ((near, (0, 3)), (away, (1, 2))):
        for s in siblings_of:
            rows = slice(s * slab, (s + 1) * slab)
            ref[rows, :] = ref[rows, :] + b[s, :, n:]


def middle(inv_own, inv_far, cp, b):
    n = inv_own.shape[0]
    count = b.shape[0] * b.shape[1]
    square = jax.ShapeDtypeStruct((n, n), jnp.float32)
    return pl.pallas_call(
        middle_kernel,
        out_shape=[jax.ShapeDtypeStruct((n, 2 * n), jnp.float32)]
        + [square] * 3
        + [jax.ShapeDtypeStruct((count, n), jnp.float32)] * 2,
        in_specs=[pl.BlockSpec(memory_space=pltpu.VMEM)] * 7,
        out_specs=[pl.BlockSpec(memory_space=pltpu.VMEM)] * 6,
        scratch_shapes=[pltpu.VMEM((3, n, n), jnp.bfloat16)] * 4,
        compiler_params=pltpu.CompilerParams(vmem_limit_bytes=48 * 1024 * 1024),
        cost_estimate=pl.CostEstimate(flops=2 * 10**10, bytes_accessed=10**7, transcendentals=0),
        name="middle",
    )(inv_own, inv_far, *cp, b)


def odd_kernel(half_ref, corner, across, corner_far, near, away, *refs):
    (own, partner, opposite, mate), (rhs_ref, mat_ref, row_ref) = refs[:4], refs[4:]
    n = corner.shape[0]
    h = n // 2
    order = 2 * n
    steps = order // BLOCK
    mat_ref[:n, :n] = -corner[...]
    mat_ref[:n, n:order] = -across[...]
    mat_ref[n:, :n] = -across[...].T
    mat_ref[n:, n:order] = -corner_far[...]
    for far, same, piece in ((0, 1, own), (0, 0, mate), (1, 1, opposite), (1, 0, partner)):
        side = half_ref[0] if same else 1 - half_ref[0]
        rows = slice(far * n, (far + 1) * n)
        cols = pl.ds(pl.multiple_of(far * n + side * h, h), h)
        mat_ref[rows, cols] = mat_ref[rows, cols] + piece[...]
    mat_ref[:n, order:] = near[...].T
    mat_ref[n:, order:] = away[...].T
    diag = mat_ref[:BLOCK, :BLOCK]
    def eliminate(k, m):
        ks = slice(k * BLOCK, (k + 1) * BLOCK)
        rest = slice((k + 1) * BLOCK, mat_ref.shape[1])
        ms = pl.ds(pl.multiple_of(m * BLOCK, BLOCK), BLOCK)
        col = wide_left(jnp.where(m == k, 0.0, mat_ref[ms, ks]))
        mat_ref[ms, rest] = mat_ref[ms, rest] - product_wide(col, row_ref[:, rest])

    width = BLOCK // 2
    share = steps * width // BLOCK
    for k in range(steps):
        ks = slice(k * BLOCK, (k + 1) * BLOCK)
        rest = slice((k + 1) * BLOCK, mat_ref.shape[1])

        def beside(p, k=k):
            for i in range(share):
                eliminate(k - 1, p * share + i)

        (inverse,) = invert_blocks([diag], width, beside if k else None)
        row = product_wide(wide_left(inverse), wide_right(mat_ref[ks, rest]))
        row_ref[:, rest] = wide_right(row)
        if k + 1 < steps:
            nxt = slice((k + 1) * BLOCK, (k + 2) * BLOCK)
            diag = mat_ref[nxt, nxt] - product_wide(wide_left(mat_ref[nxt, ks]), row_ref[:, nxt])
        mat_ref[ks, rest] = row

    def last(m, carry):
        eliminate(steps - 1, m)
        return carry

    lax.fori_loop(0, steps, last, 0)
    rhs_ref[...] = mat_ref[:, order:]


def odd_solve(half, blocks, pieces):
    order = 2 * blocks[0].shape[0]
    count = blocks[3].shape[0]
    return pl.pallas_call(
        odd_kernel,
        out_shape=jax.ShapeDtypeStruct((order, count), jnp.float32),
        in_specs=[pl.BlockSpec(memory_space=pltpu.SMEM)]
        + [pl.BlockSpec(memory_space=pltpu.VMEM)] * 9,
        out_specs=pl.BlockSpec(memory_space=pltpu.VMEM),
        scratch_shapes=[
            pltpu.VMEM((order, order + count), jnp.float32),
            pltpu.VMEM((3 * BLOCK, order + count), jnp.bfloat16),
        ],
        compiler_params=pltpu.CompilerParams(vmem_limit_bytes=40 * 1024 * 1024),
        cost_estimate=pl.CostEstimate(flops=10**10, bytes_accessed=10**8, transcendentals=0),
        name="odd_solve",
    )(half, *blocks, *pieces)


def sibling(piece, x):
    return lax.ppermute(piece, "child", [(i, i ^ x) for i in range(4)])


def siblings(piece):
    return [piece] + [sibling(piece, x) for x in range(1, 4)]


def tiles(piece):
    count = lax.axis_size("tile")
    stack = jnp.broadcast_to(piece[None], (count,) + piece.shape)
    stack = lax.all_to_all(stack, "tile", 0, 0, tiled=False)
    return stack.reshape(count * piece.shape[0], piece.shape[1])


def by_relation(stack, pos):
    pick = [jnp.where(pos == 0, stack[i], 0.0) for i in range(4)]
    for x in range(1, 4):
        pick = [jnp.where(pos == x, stack[i ^ x], pick[i]) for i in range(4)]
    return jnp.stack(pick)


def on_device(children):
    own = children[0]
    n = own.shape[2] // 4
    h = n // 2
    slab = own.shape[1]
    pos = lax.axis_index("child")
    is_even = pos % 2 == 0

    def halves(piece, keep_first):
        keep = jnp.where(keep_first, piece[:, :h], piece[:, h:])
        give = jnp.where(keep_first, piece[:, h:], piece[:, :h])
        return keep, give

    ev_rows = jnp.where(is_even, own[0], own[1])
    od_rows = jnp.where(is_even, own[1], own[0])
    ev_diag = jnp.where(is_even, ev_rows[:, :n], ev_rows[:, n : 2 * n])
    od_diag = jnp.where(is_even, od_rows[:, n : 2 * n], od_rows[:, :n])
    couple = jnp.where(is_even, ev_rows[:, n : 2 * n], ev_rows[:, :n])
    points = own[2:, :, : 2 * n].reshape(2 * slab, 2 * n)
    points = jnp.where(is_even, points, jnp.concatenate([points[:, n:], points[:, :n]], axis=1))
    border = jnp.stack([ev_rows[:, 2 * n :], od_rows[:, 2 * n :]])
    ev_keep, ev_give = halves(ev_diag, is_even)
    od_keep, od_give = halves(od_diag, is_even)
    ev = ev_keep + lax.ppermute(ev_give, "child", [(i, i ^ 1) for i in range(4)])
    od = od_keep + lax.ppermute(od_give, "child", [(i, i ^ 3) for i in range(4)])
    ev, od = lax.optimization_barrier((ev, od))
    b = lax.all_gather(points, "child", axis=0, tiled=False)
    ev = tiles(ev)
    ev, couple, border = lax.optimization_barrier((ev, couple, border))
    border = lax.all_gather(border, "tile", axis=0, tiled=True)
    half = (pos % 2).astype(jnp.int32).reshape(1)
    partner = sibling(ev, 1)
    cp = tiles(couple)
    ev, partner = lax.optimization_barrier((ev, partner))
    opposite, mate = sibling(ev, 2), sibling(ev, 3)
    inv_own = even_inverse(half, ev, partner)
    inv_own, opposite, mate, cp, od = lax.optimization_barrier((inv_own, opposite, mate, cp, od))
    cp = siblings(cp)
    b = by_relation(b, pos)
    inv_far = even_inverse(half, opposite, mate)
    od = siblings(tiles(od))

    k_own, *blocks = middle(inv_own, inv_far, cp, b)
    wo = odd_solve(half, blocks, od)
    be_own = jnp.concatenate([b[0][:, :n], b[1][:, :n]], axis=0)
    we = product_high(inv_own, be_own.T)
    we = jnp.concatenate([we, jnp.zeros((n, 4 * slab), jnp.float32)], axis=1)
    we = we - product_high(k_own, wo)
    w = jnp.stack([we, wo[:n]]).reshape(2, n // slab, slab, 8 * slab).transpose(1, 0, 2, 3)
    prod = product_left_t(w.reshape(2 * n, 8 * slab), border.reshape(2 * n, 2 * n))
    prod = prod.reshape(4, 2, slab, 2 * n)
    own_map = own[2:, :, 2 * n :]
    res = jnp.concatenate([(own_map - prod[0])[None], -prod[1:]], axis=0)
    return by_relation(res, pos).reshape(4, 2, slab, 1, 2 * n)


def solution(mesh):
    in_specs = (P(("parent", "child"), None, "tile", None),)
    out_specs = P("parent", None, "tile", "child", None)
    return jax.shard_map(
        on_device, mesh=mesh, in_specs=in_specs, out_specs=out_specs, check_vma=False
    )
```

profile of v0, /device:TPU:8, one launch (start us, length us, event | category | flops | bytes accessed | tf_op | source)
XLA Modules:
  0.0 214.6 jit_solution(2531248161406196460)
XLA Ops:
  6.5 0.0 all-gather.3.cloned.1.call-start
  6.5 1.0 slice.158
  7.5 0.7 maximum_select_fusion
  8.3 0.0 all-gather.3.cloned.1.call-update
  8.3 1.1 select_bitcast_fusion.4
  9.4 1.7 collective-permute-start.1
  11.1 2.0 collective-permute-start
  13.1 0.3 collective-permute-done.1
  13.4 1.7 collective-permute-done
  15.1 0.8 broadcast_in_dim.35
  16.0 11.0 %all-to-all-start = ((f32[16,32,256]{2,1,0:T(8,128)}), f32[16,32,256]{2,1,0:T(8,128)S(1)}, u32[]{:S(2)}, u32[]{:S(2)}) async-start(f32[16,32,256]{2,1,0:T(8,128)} %broadcast_in_dim.35), calls=%async_computation | async-start | bytes 1048576 | tf_op jit(solution)/shard_map/all_to_all | solution.py:294
  27.0 0.0 all-gather.5.cloned.1.call-start
  27.1 0.7 pad_maximum_fusion.3
  27.8 16.9 %all-to-all-done = f32[16,32,256]{2,1,0:T(8,128)S(1)} async-done(((f32[16,32,256]{2,1,0:T(8,128)}), f32[16,32,256]{2,1,0:T(8,128)S(1)}, u32[]{:S(2)}, u32[]{:S(2)}) %all-to-all-start) | async-done | bytes 524320 | tf_op jit(solution)/shard_map/all_to_all | solution.py:294
  44.7 0.0 all-gather.5.cloned.1.call-update
  44.8 1.6 collective-permute-start.2
  46.4 1.1 broadcast_in_dim.36
  47.5 4.3 %all-to-all-start.1 = ((f32[16,32,512]{2,1,0:T(8,128)}), f32[16,32,512]{2,1,0:T(8,128)}, u32[]{:S(2)}, u32[]{:S(2)}) async-start(f32[16,32,512]{2,1,0:T(8,128)} %broadcast_in_dim.36), calls=%async_computation.1 | async-start | bytes 2097152 | tf_op jit(solution)/shard_map/all_to_all | solution.py:294
  51.8 3.5 %collective-permute-done.2.other_ref = f32[512,256]{1,0:T(8,128)S(1)} collective-permute-done((f32[512,256]{1,0:T(8,128)S(1)}, f32[512,256]{1,0:T(8,128)S(1)}, u32[]{:S(2)}, u32[]{:S(2)}) %collective-permute-start.2) | collective-permute-done | bytes 524320 | tf_op jit(solution)/shard_map/ppermute | solution.py:284
  55.3 3.5 %collective-permute-start.3 = (f32[512,256]{1,0:T(8,128)S(1)}, f32[512,256]{1,0:T(8,128)S(1)}, u32[]{:S(2)}, u32[]{:S(2)}) collective-permute-start(f32[512,256]{1,0:T(8,128)S(1)} %bitcast.59), channel_id=1, source_target_pairs={{0,32},{16,48},{32,0},{48,16},{1,33},{17,49},{33,1},{49,17},{2,34}... | collective-permute-start | bytes 1572872 | tf_op jit(solution)/shard_map/ppermute | solution.py:284
  58.9 0.8 collective-permute-start.4
  59.7 20.7 %even_inverse.2.inv_own = f32[512,512]{1,0:T(8,128)S(1)} custom-call(s32[1]{0:T(128)} %bitcast.half_ref, f32[512,256]{1,0:T(8,128)S(1)} %bitcast.61, f32[512,256]{1,0:T(8,128)S(1)} %collective-permute-done.2.other_ref), custom_call_target="tpu_custom_call" | custom-call | flops 10000000000 | bytes 100000000 | tf_op jit(solution)/shard_map/even_inverse/pallas_call | solution.py:136
  80.5 0.0 all-gather.3.cloned.1.call-done
  80.5 1.4 slice_bitcast_fusion
  81.9 1.3 slice_bitcast_fusion.3
  83.1 1.0 pad_maximum_fusion.b
  84.2 0.0 collective-permute-done.3.mine_ref
  84.2 0.0 collective-permute-done.4.other_ref
  84.3 1.4 all-to-all-done.1
  85.7 0.5 collective-permute-start.5
  86.1 2.0 collective-permute-start.6
  88.2 1.0 collective-permute-start.7
  89.2 0.9 broadcast_in_dim.39
  90.0 3.9 %all-to-all-start.2 = ((f32[16,32,256]{2,1,0:T(8,128)}), f32[16,32,256]{2,1,0:T(8,128)S(1)}, u32[]{:S(2)}, u32[]{:S(2)}) async-start(f32[16,32,256]{2,1,0:T(8,128)} %broadcast_in_dim.39), calls=%async_computation.2 | async-start | bytes 1048576 | tf_op jit(solution)/shard_map/all_to_all | solution.py:294
  93.9 1.0 fusion
  94.9 20.8 %even_inverse.3.inv_far = f32[512,512]{1,0:T(8,128)S(1)} custom-call(s32[1]{0:T(128)} %bitcast.half_ref, f32[512,256]{1,0:T(8,128)S(1)} %collective-permute-done.3.mine_ref, f32[512,256]{1,0:T(8,128)S(1)} %collective-permute-done.4.other_ref), custom_call_target="tpu_custom_call" | custom-call | flops 10000000000 | bytes 100000000 | tf_op jit(solution)/shard_map/even_inverse/pallas_call | solution.py:136
  115.6 0.0 copy-start
  115.7 1.0 copy-done
  116.6 0.0 all-to-all-done.2
  116.6 1.1 collective-permute-start.10
  117.7 3.7 %collective-permute-start.8 = (f32[512,256]{1,0:T(8,128)S(1)}, f32[512,256]{1,0:T(8,128)S(1)}, u32[]{:S(2)}, u32[]{:S(2)}) collective-permute-start(f32[512,256]{1,0:T(8,128)S(1)} %bitcast.63), channel_id=1, source_target_pairs={{0,16},{16,0},{32,48},{48,32},{1,17},{17,1},{33,49},{49,33},{2,18}... | collective-permute-start | bytes 1572872 | tf_op jit(solution)/shard_map/ppermute | solution.py:284
  121.5 0.0 collective-permute-done.5.c1
  121.5 0.6 collective-permute-start.9
  122.0 13.1 %collective-permute-done.6.c2 = f32[512,512]{1,0:T(8,128)} collective-permute-done((f32[512,512]{1,0:T(8,128)}, f32[512,512]{1,0:T(8,128)}, u32[]{:S(2)}, u32[]{:S(2)}) %collective-permute-start.6) | collective-permute-done | bytes 1048608 | tf_op jit(solution)/shard_map/ppermute | solution.py:284
  135.1 0.0 collective-permute-done.7.c3
  135.1 20.6 %middle.1 = (f32[512,1024]{1,0:T(8,128)}, f32[512,512]{1,0:T(8,128)S(1)}, f32[512,512]{1,0:T(8,128)S(1)}, f32[512,512]{1,0:T(8,128)S(1)}, f32[256,512]{1,0:T(8,128)S(1)}, /*index=5*/f32[256,512]{1,0:T(8,128)S(1)}) custom-call(f32[512,512]{1,0:T(8,128)S(1)} %even_inverse.2.inv_own, f32[512,512]{1,0:T(8,128)} %copy-done, f32[512,512]{1,0:T(8,128)} %bitcast.6.c0, ...), custom_call_target="tpu_custom_call" | custom-call | flops 20000000000 | bytes 10000000 | tf_op jit(solution)/shard_map/middle/pallas_call | solution.py:199
  155.8 0.0 collective-permute-done.10.refs_3_
  155.8 0.0 collective-permute-done.8.refs_1_
  155.8 0.0 collective-permute-done.9.refs_2_
  155.8 0.0 copy-start.1
  155.8 42.5 %odd_solve.1 = f32[1024,256]{1,0:T(8,128)S(1)} custom-call(s32[1]{0:T(128)} %bitcast.half_ref, f32[512,512]{1,0:T(8,128)S(1)} %get-tuple-element.34.corner, f32[512,512]{1,0:T(8,128)S(1)} %get-tuple-element.35.across, f32[512,512]{1,0:T(8,128)S(1)} %get-tuple-element.36.corner_far, f32[256,512]{1,0:T(8,128)S(1)} %get-tuple-element.37.near, ...), custom_call_target="tpu_custom_call" | custom-call | flops 10000000000 | bytes 100000000 | tf_op jit(solution)/shard_map/odd_solve/pallas_call | solution.py:267
  198.3 0.0 copy-done.1
  198.4 1.8 pad_subtract_fusion
  200.2 0.1 pad_maximum_fusion.1
  200.3 0.0 all-gather.5.cloned.1.call-done
  200.3 4.1 %fusion.6 = f32[256,1024]{1,0:T(8,128)S(1)} fusion(f32[1024,256]{1,0:T(8,128)S(1)} %bitcast.67, f32[1024,1024]{1,0:T(8,128)} %bitcast.66), kind=kOutput, calls=%fused_computation.41 | convolution fusion | flops 1610612736 | bytes 6291456 | tf_op jit(solution)/shard_map/dot_general | solution.py:18
  204.4 0.1 slice_negate_fusion
  204.5 0.1 fusion.5
  204.6 1.0 select_bitcast_fusion.3
  205.6 0.1 select_bitcast_fusion.2
  205.8 0.1 pad_maximum_fusion.2
  205.9 1.7 reshape.97
  (11 shorter events, 0.2 us)
Async XLA Ops:
  6.5 73.9 %all-gather.3.cloned.1.call-start = ((), (), s32[]{:S(2)}) async-start(), calls=%async_computation.3 | async-start | bytes 1310720 | tf_op jit(solution)/shard_map/all_gather | solution.py:331
  9.4 4.0 %collective-permute-start.1 = (f32[32,256]{1,0:T(8,128)S(1)}, f32[32,256]{1,0:T(8,128)S(1)}, u32[]{:S(2)}, u32[]{:S(2)}) collective-permute-start(f32[32,256]{1,0:T(8,128)S(1)} %slice_select_fusion.3), channel_id=1, source_target_pairs={{0,48},{16,32},{32,16},{48,0},{1,49},{17,33},{33,17},{49,1},{2,50}... | collective-permute-start | bytes 98312 | tf_op jit(solution)/shard_map/ppermute | solution.py:329
  11.1 4.0 %collective-permute-start = (f32[32,256]{1,0:T(8,128)S(1)}, f32[32,256]{1,0:T(8,128)S(1)}, u32[]{:S(2)}, u32[]{:S(2)}) collective-permute-start(f32[32,256]{1,0:T(8,128)S(1)} %slice_select_fusion.4), channel_id=1, source_target_pairs={{0,16},{16,0},{32,48},{48,32},{1,17},{17,1},{33,49},{49,33},{2,18}... | collective-permute-start | bytes 98312 | tf_op jit(solution)/shard_map/ppermute | solution.py:328
  16.0 28.8 %all-to-all-start = ((f32[16,32,256]{2,1,0:T(8,128)}), f32[16,32,256]{2,1,0:T(8,128)S(1)}, u32[]{:S(2)}, u32[]{:S(2)}) async-start(f32[16,32,256]{2,1,0:T(8,128)} %broadcast_in_dim.35), calls=%async_computation | async-start | bytes 1048576 | tf_op jit(solution)/shard_map/all_to_all | solution.py:294
  27.0 173.3 %all-gather.5.cloned.1.call-start = ((), (), s32[]{:S(2)}) async-start(), calls=%async_computation.4 | async-start | bytes 4456448 | tf_op jit(solution)/shard_map/all_gather | solution.py:334
  44.8 10.6 %collective-permute-start.2 = (f32[512,256]{1,0:T(8,128)S(1)}, f32[512,256]{1,0:T(8,128)S(1)}, u32[]{:S(2)}, u32[]{:S(2)}) collective-permute-start(f32[512,256]{1,0:T(8,128)S(1)} %bitcast.58), channel_id=1, source_target_pairs={{0,16},{16,0},{32,48},{48,32},{1,17},{17,1},{33,49},{49,33},{2,18}... | collective-permute-start | bytes 1572872 | tf_op jit(solution)/shard_map/ppermute | solution.py:284
  47.5 38.2 %all-to-all-start.1 = ((f32[16,32,512]{2,1,0:T(8,128)}), f32[16,32,512]{2,1,0:T(8,128)}, u32[]{:S(2)}, u32[]{:S(2)}) async-start(f32[16,32,512]{2,1,0:T(8,128)} %broadcast_in_dim.36), calls=%async_computation.1 | async-start | bytes 2097152 | tf_op jit(solution)/shard_map/all_to_all | solution.py:294
  55.3 28.9 %collective-permute-start.3 = (f32[512,256]{1,0:T(8,128)S(1)}, f32[512,256]{1,0:T(8,128)S(1)}, u32[]{:S(2)}, u32[]{:S(2)}) collective-permute-start(f32[512,256]{1,0:T(8,128)S(1)} %bitcast.59), channel_id=1, source_target_pairs={{0,32},{16,48},{32,0},{48,16},{1,33},{17,49},{33,1},{49,17},{2,34}... | collective-permute-start | bytes 1572872 | tf_op jit(solution)/shard_map/ppermute | solution.py:284
  58.9 25.4 %collective-permute-start.4 = (f32[512,256]{1,0:T(8,128)S(1)}, f32[512,256]{1,0:T(8,128)S(1)}, u32[]{:S(2)}, u32[]{:S(2)}) collective-permute-start(f32[512,256]{1,0:T(8,128)S(1)} %bitcast.60), channel_id=1, source_target_pairs={{0,48},{16,32},{32,16},{48,0},{1,49},{17,33},{33,17},{49,1},{2,50}... | collective-permute-start | bytes 1572872 | tf_op jit(solution)/shard_map/ppermute | solution.py:284
  85.7 35.8 %collective-permute-start.5 = (f32[512,512]{1,0:T(8,128)}, f32[512,512]{1,0:T(8,128)}, u32[]{:S(2)}, u32[]{:S(2)}) collective-permute-start(f32[512,512]{1,0:T(8,128)} %bitcast.6.c0), channel_id=1, source_target_pairs={{0,16},{16,0},{32,48},{48,32},{1,17},{17,1},{33,49},{49,33},{2,18}... | collective-permute-start | bytes 3145736 | tf_op jit(solution)/shard_map/ppermute | solution.py:284
  86.1 49.0 %collective-permute-start.6 = (f32[512,512]{1,0:T(8,128)}, f32[512,512]{1,0:T(8,128)}, u32[]{:S(2)}, u32[]{:S(2)}) collective-permute-start(f32[512,512]{1,0:T(8,128)} %bitcast.6.c0), channel_id=1, source_target_pairs={{0,32},{16,48},{32,0},{48,16},{1,33},{17,49},{33,1},{49,17},{2,34}... | collective-permute-start | bytes 3145736 | tf_op jit(solution)/shard_map/ppermute | solution.py:284
  88.2 47.0 %collective-permute-start.7 = (f32[512,512]{1,0:T(8,128)}, f32[512,512]{1,0:T(8,128)}, u32[]{:S(2)}, u32[]{:S(2)}) collective-permute-start(f32[512,512]{1,0:T(8,128)} %bitcast.6.c0), channel_id=1, source_target_pairs={{0,48},{16,32},{32,16},{48,0},{1,49},{17,33},{33,17},{49,1},{2,50}... | collective-permute-start | bytes 3145736 | tf_op jit(solution)/shard_map/ppermute | solution.py:284
  90.0 26.6 %all-to-all-start.2 = ((f32[16,32,256]{2,1,0:T(8,128)}), f32[16,32,256]{2,1,0:T(8,128)S(1)}, u32[]{:S(2)}, u32[]{:S(2)}) async-start(f32[16,32,256]{2,1,0:T(8,128)} %broadcast_in_dim.39), calls=%async_computation.2 | async-start | bytes 1048576 | tf_op jit(solution)/shard_map/all_to_all | solution.py:294
  115.6 1.0 copy-start
  116.6 39.1 %collective-permute-start.10 = (f32[512,256]{1,0:T(8,128)S(1)}, f32[512,256]{1,0:T(8,128)S(1)}, u32[]{:S(2)}, u32[]{:S(2)}) collective-permute-start(f32[512,256]{1,0:T(8,128)S(1)} %bitcast.62), channel_id=1, source_target_pairs={{0,48},{16,32},{32,16},{48,0},{1,49},{17,33},{33,17},{49,1},{2,50}... | collective-permute-start | bytes 1572872 | tf_op jit(solution)/shard_map/ppermute | solution.py:284
  117.7 38.0 %collective-permute-start.8 = (f32[512,256]{1,0:T(8,128)S(1)}, f32[512,256]{1,0:T(8,128)S(1)}, u32[]{:S(2)}, u32[]{:S(2)}) collective-permute-start(f32[512,256]{1,0:T(8,128)S(1)} %bitcast.63), channel_id=1, source_target_pairs={{0,16},{16,0},{32,48},{48,32},{1,17},{17,1},{33,49},{49,33},{2,18}... | collective-permute-start | bytes 1572872 | tf_op jit(solution)/shard_map/ppermute | solution.py:284
  121.5 34.3 %collective-permute-start.9 = (f32[512,256]{1,0:T(8,128)S(1)}, f32[512,256]{1,0:T(8,128)S(1)}, u32[]{:S(2)}, u32[]{:S(2)}) collective-permute-start(f32[512,256]{1,0:T(8,128)S(1)} %bitcast.64), channel_id=1, source_target_pairs={{0,32},{16,48},{32,0},{48,16},{1,33},{17,49},{33,1},{49,17},{2,34}... | collective-permute-start | bytes 1572872 | tf_op jit(solution)/shard_map/ppermute | solution.py:284
  155.8 42.6 %copy-start.1 = (f32[512,1024]{1,0:T(8,128)S(1)}, f32[512,1024]{1,0:T(8,128)}, u32[]{:S(2)}) copy-start(f32[512,1024]{1,0:T(8,128)} %get-tuple-element.33) | copy-start | bytes 6291460
Sparse Core Ops, SparseCore 0:
  9.2 28.4 all-gather.2
  44.9 105.4 all-gather.4
where the time goes:
time: 218 us; the launch traced here: 215 us
  Pallas kernels  105 us (48%)
  starting transfers between devices  37.8 us (17%)
  waiting for transfers between devices  37 us (17%)
  between operations  13.9 us (6%)
  other arithmetic  7.72 us (4%)
  matrix products  6.91 us (3%)
  local copies, waits for them, and re-layouts  6.6 us (3%)
    pallas_call x1, Pallas kernels, odd_solve(): pl.pallas_call(odd_kernel, out_shape=jax.ShapeDtypeStruct((order, count),...  42.5 us
    pallas_call x2, Pallas kernels, even_inverse(): pl.pallas_call(even_kernel, out_shape=jax.ShapeDtypeStruct((n, n), jnp.fl...  41.5 us
    pallas_call x1, Pallas kernels, middle(): pl.pallas_call(middle_kernel, out_shape=[jax.ShapeDtypeStruct((n, 2 * n),...  20.6 us
    all_to_all x3, starting transfers between devices, tiles(): stack = lax.all_to_all(stack, 'tile', 0, 0, tiled=False)  19.2 us
    all_to_all x3, waiting for transfers between devices, tiles(): stack = lax.all_to_all(stack, 'tile', 0, 0, tiled=False)  18.3 us
    ppermute x9, waiting for transfers between devices, sibling(): return lax.ppermute(piece, 'child', [(i, i ^ x) for i in range(4)])  16.6 us
    ppermute x9, starting transfers between devices, sibling(): return lax.ppermute(piece, 'child', [(i, i ^ x) for i in range(4)])  14.9 us
  transfers between devices with their start and end apart: 16, of which 6 were waited for; matrix products, arithmetic and copies ran while one was open for 5% of the time, Pallas kernels for 49%

commit v1 on v0

--- a/solution.py
+++ b/solution.py
@@ -145,11 +145,11 @@
     )(half, mine, other)
 
 
-def middle_kernel(
-    inv_own, inv_far, c0, c1, c2, c3, b, k_own, corner, across, corner_far, near, away, w0, w1, w2, w3
-):
+def middle_kernel(pos_ref, inv_own, inv_far, c0, c1, c2, c3, b_ref, *refs):
+    k_own, corner, across, corner_far, near, away, reach, w0, w1, w2, w3 = refs
+    b = [b_ref[jnp.bitwise_xor(pos_ref[0], s)] for s in range(4)]
     n = corner.shape[0]
-    slab = b.shape[1]
+    slab = b_ref.shape[1]
 
     def chunk(m):
         return pl.ds(pl.multiple_of(m * BLOCK, BLOCK), BLOCK)
@@ -179,8 +179,10 @@
         return carry
 
     lax.fori_loop(0, n // BLOCK, schur, 0)
-    own = wide_left(jnp.concatenate([b[0, :, :n], b[1, :, :n]], axis=0))
-    far = wide_left(jnp.concatenate([b[2, :, :n], b[3, :, :n]], axis=0))
+    be_own = jnp.concatenate([b[0][:, :n], b[1][:, :n]], axis=0)
+    own = wide_left(be_own)
+    far = wide_left(jnp.concatenate([b[2][:, :n], b[3][:, :n]], axis=0))
+    reach[...] = product_high(inv_own[...], be_own.T)
     half = 2 * slab
     near[:half, :] = -product_wide(own, r0)
     near[half:, :] = -product_wide(far, r3)
@@ -189,10 +191,10 @@
     for ref, siblings_of in ((near, (0, 3)), (away, (1, 2))):
         for s in siblings_of:
             rows = slice(s * slab, (s + 1) * slab)
-            ref[rows, :] = ref[rows, :] + b[s, :, n:]
-
-
-def middle(inv_own, inv_far, cp, b):
+            ref[rows, :] = ref[rows, :] + b[s][:, n:]
+
+
+def middle(pos, inv_own, inv_far, cp, b):
     n = inv_own.shape[0]
     count = b.shape[0] * b.shape[1]
     square = jax.ShapeDtypeStruct((n, n), jnp.float32)
@@ -200,14 +202,16 @@
         middle_kernel,
         out_shape=[jax.ShapeDtypeStruct((n, 2 * n), jnp.float32)]
         + [square] * 3
-        + [jax.ShapeDtypeStruct((count, n), jnp.float32)] * 2,
-        in_specs=[pl.BlockSpec(memory_space=pltpu.VMEM)] * 7,
-        out_specs=[pl.BlockSpec(memory_space=pltpu.VMEM)] * 6,
+        + [jax.ShapeDtypeStruct((count, n), jnp.float32)] * 2
+        + [jax.ShapeDtypeStruct((n, count // 2), jnp.float32)],
+        in_specs=[pl.BlockSpec(memory_space=pltpu.SMEM)]
+        + [pl.BlockSpec(memory_space=pltpu.VMEM)] * 7,
+        out_specs=[pl.BlockSpec(memory_space=pltpu.VMEM)] * 7,
         scratch_shapes=[pltpu.VMEM((3, n, n), jnp.bfloat16)] * 4,
         compiler_params=pltpu.CompilerParams(vmem_limit_bytes=48 * 1024 * 1024),
         cost_estimate=pl.CostEstimate(flops=2 * 10**10, bytes_accessed=10**7, transcendentals=0),
         name="middle",
-    )(inv_own, inv_far, *cp, b)
+    )(pos, inv_own, inv_far, *cp, b)
 
 
 def odd_kernel(half_ref, corner, across, corner_far, near, away, *refs):
@@ -340,14 +344,11 @@
     inv_own = even_inverse(half, ev, partner)
     inv_own, opposite, mate, cp, od = lax.optimization_barrier((inv_own, opposite, mate, cp, od))
     cp = siblings(cp)
-    b = by_relation(b, pos)
     inv_far = even_inverse(half, opposite, mate)
     od = siblings(tiles(od))
 
-    k_own, *blocks = middle(inv_own, inv_far, cp, b)
+    k_own, *blocks, we = middle(pos.astype(jnp.int32).reshape(1), inv_own, inv_far, cp, b)
     wo = odd_solve(half, blocks, od)
-    be_own = jnp.concatenate([b[0][:, :n], b[1][:, :n]], axis=0)
-    we = product_high(inv_own, be_own.T)
     we = jnp.concatenate([we, jnp.zeros((n, 4 * slab), jnp.float32)], axis=1)
     we = we - product_high(k_own, wo)
     w = jnp.stack([we, wo[:n]]).reshape(2, n // slab, slab, 8 * slab).transpose(1, 0, 2, 3)

time: 218 us -> 222 us (1.018)
  the two profiles are of different devices: /device:TPU:8 before, /device:TPU:6 now
where the time goes in v1:
time: 222 us; the launch traced here: 218 us
  Pallas kernels  105 us (47%)
  starting transfers between devices  45.7 us (21%)
  waiting for transfers between devices  36.4 us (16%)
  between operations  13.9 us (6%)
  local copies, waits for them, and re-layouts  6.59 us (3%)
  matrix products  5.93 us (3%)
  other arithmetic  4 us (2%)
    pallas_call x1, Pallas kernels, odd_solve(): pl.pallas_call(odd_kernel, out_shape=jax.ShapeDtypeStruct((order, count),...  42.4 us
    pallas_call x2, Pallas kernels, even_inverse(): pl.pallas_call(even_kernel, out_shape=jax.ShapeDtypeStruct((n, n), jnp.fl...  41.5 us
    all_to_all x3, starting transfers between devices, tiles(): stack = lax.all_to_all(stack, 'tile', 0, 0, tiled=False)  29.1 us
    pallas_call x1, Pallas kernels, middle(): pl.pallas_call(middle_kernel, out_shape=[jax.ShapeDtypeStruct((n, 2 * n),...  21.6 us
    ppermute x9, waiting for transfers between devices, sibling(): return lax.ppermute(piece, 'child', [(i, i ^ x) for i in range(4)])  19.1 us
    all_to_all x3, waiting for transfers between devices, tiles(): stack = lax.all_to_all(stack, 'tile', 0, 0, tiled=False)  13.4 us
    ppermute x9, starting transfers between devices, sibling(): return lax.ppermute(piece, 'child', [(i, i ^ x) for i in range(4)])  13.2 us
  transfers between devices with their start and end apart: 16, of which 6 were waited for; matrix products, arithmetic and copies ran while one was open for 3% of the time, Pallas kernels for 48%

profile of v1, /device:TPU:6, one launch (start us, length us, event | category | flops | bytes accessed | tf_op | source)
XLA Modules:
  0.0 218.0 jit_solution(10798349630972385412)
XLA Ops:
  6.5 0.0 all-gather.3.cloned.1.call-start
  6.5 1.1 select_bitcast_fusion.4
  7.6 3.1 %collective-permute-start.1 = (f32[32,256]{1,0:T(8,128)S(1)}, f32[32,256]{1,0:T(8,128)S(1)}, u32[]{:S(2)}, u32[]{:S(2)}) collective-permute-start(f32[32,256]{1,0:T(8,128)S(1)} %slice_select_fusion.3), channel_id=1, source_target_pairs={{0,48},{16,32},{32,16},{48,0},{1,49},{17,33},{33,17},{49,1},{2,50}... | collective-permute-start | bytes 98312 | tf_op jit(solution)/shard_map/ppermute | solution.py:333
  10.7 1.0 slice.122
  11.7 0.8 maximum_select_fusion
  12.5 0.0 all-gather.3.cloned.1.call-update
  12.6 0.2 collective-permute-start
  12.8 0.1 collective-permute-done.1
  12.9 3.7 %collective-permute-done = f32[32,256]{1,0:T(8,128)S(1)} collective-permute-done((f32[32,256]{1,0:T(8,128)S(1)}, f32[32,256]{1,0:T(8,128)S(1)}, u32[]{:S(2)}, u32[]{:S(2)}) %collective-permute-start) | collective-permute-done | bytes 32800 | tf_op jit(solution)/shard_map/ppermute | solution.py:332
  16.6 0.8 broadcast_in_dim.12
  17.4 11.4 %all-to-all-start = ((f32[16,32,256]{2,1,0:T(8,128)}), f32[16,32,256]{2,1,0:T(8,128)S(1)}, u32[]{:S(2)}, u32[]{:S(2)}) async-start(f32[16,32,256]{2,1,0:T(8,128)} %broadcast_in_dim.12), calls=%async_computation | async-start | bytes 1048576 | tf_op jit(solution)/shard_map/all_to_all | solution.py:298
  28.9 0.0 all-gather.5.cloned.1.call-start
  28.9 0.7 pad_maximum_fusion.2
  29.7 13.4 %all-to-all-done = f32[16,32,256]{2,1,0:T(8,128)S(1)} async-done(((f32[16,32,256]{2,1,0:T(8,128)}), f32[16,32,256]{2,1,0:T(8,128)S(1)}, u32[]{:S(2)}, u32[]{:S(2)}) %all-to-all-start) | async-done | bytes 524320 | tf_op jit(solution)/shard_map/all_to_all | solution.py:298
  43.1 0.0 all-gather.5.cloned.1.call-update
  43.1 1.1 broadcast_in_dim.13
  44.2 7.3 %all-to-all-start.1 = ((f32[16,32,512]{2,1,0:T(8,128)}), f32[16,32,512]{2,1,0:T(8,128)}, u32[]{:S(2)}, u32[]{:S(2)}) async-start(f32[16,32,512]{2,1,0:T(8,128)} %broadcast_in_dim.13), calls=%async_computation.1 | async-start | bytes 2097152 | tf_op jit(solution)/shard_map/all_to_all | solution.py:298
  51.5 0.5 collective-permute-start.2
  52.0 11.4 %collective-permute-done.2.other_ref = f32[512,256]{1,0:T(8,128)S(1)} collective-permute-done((f32[512,256]{1,0:T(8,128)S(1)}, f32[512,256]{1,0:T(8,128)S(1)}, u32[]{:S(2)}, u32[]{:S(2)}) %collective-permute-start.2) | collective-permute-done | bytes 524320 | tf_op jit(solution)/shard_map/ppermute | solution.py:288
  63.4 0.0 collective-permute-start.3
  63.4 3.1 %collective-permute-start.4 = (f32[512,256]{1,0:T(8,128)S(1)}, f32[512,256]{1,0:T(8,128)S(1)}, u32[]{:S(2)}, u32[]{:S(2)}) collective-permute-start(f32[512,256]{1,0:T(8,128)S(1)} %bitcast.56), channel_id=1, source_target_pairs={{0,48},{16,32},{32,16},{48,0},{1,49},{17,33},{33,17},{49,1},{2,50}... | collective-permute-start | bytes 1572872 | tf_op jit(solution)/shard_map/ppermute | solution.py:288
  66.5 20.7 %even_inverse.2.inv_own = f32[512,512]{1,0:T(8,128)S(1)} custom-call(s32[1]{0:T(128)} %bitcast.1.half_ref, f32[512,256]{1,0:T(8,128)S(1)} %bitcast.57, f32[512,256]{1,0:T(8,128)S(1)} %collective-permute-done.2.other_ref), custom_call_target="tpu_custom_call" | custom-call | flops 10000000000 | bytes 100000000 | tf_op jit(solution)/shard_map/even_inverse/pallas_call | solution.py:136
  87.2 0.0 collective-permute-done.3.mine_ref
  87.2 0.0 collective-permute-done.4.other_ref
  87.3 0.0 all-to-all-done.1
  87.3 0.8 collective-permute-start.5
  88.0 1.2 collective-permute-start.6
  89.2 2.8 %collective-permute-start.7 = (f32[512,512]{1,0:T(8,128)}, f32[512,512]{1,0:T(8,128)}, u32[]{:S(2)}, u32[]{:S(2)}) collective-permute-start(f32[512,512]{1,0:T(8,128)} %bitcast.7.c0), channel_id=1, source_target_pairs={{0,48},{16,32},{32,16},{48,0},{1,49},{17,33},{33,17},{49,1},{2,50}... | collective-permute-start | bytes 3145736 | tf_op jit(solution)/shard_map/ppermute | solution.py:288
  92.1 0.9 broadcast_in_dim.28
  92.9 10.3 %all-to-all-start.2 = ((f32[16,32,256]{2,1,0:T(8,128)}), f32[16,32,256]{2,1,0:T(8,128)S(1)}, u32[]{:S(2)}, u32[]{:S(2)}) async-start(f32[16,32,256]{2,1,0:T(8,128)} %broadcast_in_dim.28), calls=%async_computation.2 | async-start | bytes 1048576 | tf_op jit(solution)/shard_map/all_to_all | solution.py:298
  103.2 20.7 %even_inverse.3.inv_far = f32[512,512]{1,0:T(8,128)S(1)} custom-call(s32[1]{0:T(128)} %bitcast.1.half_ref, f32[512,256]{1,0:T(8,128)S(1)} %collective-permute-done.3.mine_ref, f32[512,256]{1,0:T(8,128)S(1)} %collective-permute-done.4.other_ref), custom_call_target="tpu_custom_call" | custom-call | flops 10000000000 | bytes 100000000 | tf_op jit(solution)/shard_map/even_inverse/pallas_call | solution.py:136
  124.0 0.0 copy-start
  124.0 1.0 copy-done
  125.0 0.0 all-to-all-done.2
  125.0 0.4 collective-permute-start.10
  125.4 0.0 collective-permute-start.8
  125.4 0.0 collective-permute-done.5.c1
  125.4 4.4 %collective-permute-start.9 = (f32[512,256]{1,0:T(8,128)S(1)}, f32[512,256]{1,0:T(8,128)S(1)}, u32[]{:S(2)}, u32[]{:S(2)}) collective-permute-start(f32[512,256]{1,0:T(8,128)S(1)} %bitcast.52), channel_id=1, source_target_pairs={{0,32},{16,48},{32,0},{48,16},{1,33},{17,49},{33,1},{49,17},{2,34}... | collective-permute-start | bytes 1572872 | tf_op jit(solution)/shard_map/ppermute | solution.py:288
  129.8 0.0 all-gather.3.cloned.1.call-done.b_ref
  129.8 6.3 %collective-permute-done.6.c2 = f32[512,512]{1,0:T(8,128)} collective-permute-done((f32[512,512]{1,0:T(8,128)}, f32[512,512]{1,0:T(8,128)}, u32[]{:S(2)}, u32[]{:S(2)}) %collective-permute-start.6) | collective-permute-done | bytes 1048608 | tf_op jit(solution)/shard_map/ppermute | solution.py:288
  136.1 1.4 collective-permute-done.7.c3
  137.6 21.6 %middle.1 = (f32[512,1024]{1,0:T(8,128)}, f32[512,512]{1,0:T(8,128)S(1)}, f32[512,512]{1,0:T(8,128)S(1)}, f32[512,512]{1,0:T(8,128)S(1)}, f32[256,512]{1,0:T(8,1...) custom-call(s32[1]{0:T(128)} %bitcast.pos_ref, f32[512,512]{1,0:T(8,128)S(1)} %even_inverse.2.inv_own, ...), custom_call_target="tpu_custom_call" | custom-call | flops 20000000000 | bytes 10000000 | tf_op jit(solution)/shard_map/middle/pallas_call | solution.py:201
  159.1 0.0 collective-permute-done.10.refs_3_
  159.2 0.0 collective-permute-done.8.refs_1_
  159.2 0.0 collective-permute-done.9.refs_2_
  159.2 0.0 copy-start.1
  159.2 42.4 %odd_solve.1 = f32[1024,256]{1,0:T(8,128)S(1)} custom-call(s32[1]{0:T(128)} %bitcast.1.half_ref, f32[512,512]{1,0:T(8,128)S(1)} %get-tuple-element.36.corner, f32[512,512]{1,0:T(8,128)S(1)} %get-tuple-element.37.across, f32[512,512]{1,0:T(8,128)S(1)} %get-tuple-element.38.corner_far, f32[256,512]{1,0:T(8,128)S(1)} %get-tuple-element.39.near, ...), custom_call_target="tpu_custom_call" | custom-call | flops 10000000000 | bytes 100000000 | tf_op jit(solution)/shard_map/odd_solve/pallas_call | solution.py:271
  201.6 0.0 copy-done.1
  201.6 1.8 pad_subtract_fusion
  203.5 0.1 pad_maximum_fusion
  203.5 0.0 all-gather.5.cloned.1.call-done
  203.6 4.1 %fusion.1 = f32[256,1024]{1,0:T(8,128)S(1)} fusion(f32[1024,256]{1,0:T(8,128)S(1)} %bitcast.59, f32[1024,1024]{1,0:T(8,128)} %bitcast.58), kind=kOutput, calls=%fused_computation.25 | convolution fusion | flops 1610612736 | bytes 6291456 | tf_op jit(solution)/shard_map/dot_general | solution.py:18
  207.7 0.1 slice_negate_fusion
  207.8 0.1 fusion
  207.9 1.0 select_bitcast_fusion.3
  208.9 0.1 select_bitcast_fusion.2
  209.0 0.1 pad_maximum_fusion.1
  209.2 1.7 reshape.101
  (10 shorter events, 0.1 us)
Async XLA Ops:
  6.5 123.3 %all-gather.3.cloned.1.call-start = ((), (), s32[]{:S(2)}) async-start(), calls=%async_computation.3 | async-start | bytes 1310720 | tf_op jit(solution)/shard_map/all_gather | solution.py:335
  7.6 5.2 %collective-permute-start.1 = (f32[32,256]{1,0:T(8,128)S(1)}, f32[32,256]{1,0:T(8,128)S(1)}, u32[]{:S(2)}, u32[]{:S(2)}) collective-permute-start(f32[32,256]{1,0:T(8,128)S(1)} %slice_select_fusion.3), channel_id=1, source_target_pairs={{0,48},{16,32},{32,16},{48,0},{1,49},{17,33},{33,17},{49,1},{2,50}... | collective-permute-start | bytes 98312 | tf_op jit(solution)/shard_map/ppermute | solution.py:333
  12.6 4.0 %collective-permute-start = (f32[32,256]{1,0:T(8,128)S(1)}, f32[32,256]{1,0:T(8,128)S(1)}, u32[]{:S(2)}, u32[]{:S(2)}) collective-permute-start(f32[32,256]{1,0:T(8,128)S(1)} %slice_select_fusion.4), channel_id=1, source_target_pairs={{0,16},{16,0},{32,48},{48,32},{1,17},{17,1},{33,49},{49,33},{2,18}... | collective-permute-start | bytes 98312 | tf_op jit(solution)/shard_map/ppermute | solution.py:332
  17.4 25.7 %all-to-all-start = ((f32[16,32,256]{2,1,0:T(8,128)}), f32[16,32,256]{2,1,0:T(8,128)S(1)}, u32[]{:S(2)}, u32[]{:S(2)}) async-start(f32[16,32,256]{2,1,0:T(8,128)} %broadcast_in_dim.12), calls=%async_computation | async-start | bytes 1048576 | tf_op jit(solution)/shard_map/all_to_all | solution.py:298
  28.9 174.7 %all-gather.5.cloned.1.call-start = ((), (), s32[]{:S(2)}) async-start(), calls=%async_computation.4 | async-start | bytes 4456448 | tf_op jit(solution)/shard_map/all_gather | solution.py:338
  44.2 43.1 %all-to-all-start.1 = ((f32[16,32,512]{2,1,0:T(8,128)}), f32[16,32,512]{2,1,0:T(8,128)}, u32[]{:S(2)}, u32[]{:S(2)}) async-start(f32[16,32,512]{2,1,0:T(8,128)} %broadcast_in_dim.13), calls=%async_computation.1 | async-start | bytes 2097152 | tf_op jit(solution)/shard_map/all_to_all | solution.py:298
  51.5 11.8 %collective-permute-start.2 = (f32[512,256]{1,0:T(8,128)S(1)}, f32[512,256]{1,0:T(8,128)S(1)}, u32[]{:S(2)}, u32[]{:S(2)}) collective-permute-start(f32[512,256]{1,0:T(8,128)S(1)} %bitcast.54), channel_id=1, source_target_pairs={{0,16},{16,0},{32,48},{48,32},{1,17},{17,1},{33,49},{49,33},{2,18}... | collective-permute-start | bytes 1572872 | tf_op jit(solution)/shard_map/ppermute | solution.py:288
  63.4 23.9 %collective-permute-start.3 = (f32[512,256]{1,0:T(8,128)S(1)}, f32[512,256]{1,0:T(8,128)S(1)}, u32[]{:S(2)}, u32[]{:S(2)}) collective-permute-start(f32[512,256]{1,0:T(8,128)S(1)} %bitcast.55), channel_id=1, source_target_pairs={{0,32},{16,48},{32,0},{48,16},{1,33},{17,49},{33,1},{49,17},{2,34}... | collective-permute-start | bytes 1572872 | tf_op jit(solution)/shard_map/ppermute | solution.py:288
  63.4 23.9 %collective-permute-start.4 = (f32[512,256]{1,0:T(8,128)S(1)}, f32[512,256]{1,0:T(8,128)S(1)}, u32[]{:S(2)}, u32[]{:S(2)}) collective-permute-start(f32[512,256]{1,0:T(8,128)S(1)} %bitcast.56), channel_id=1, source_target_pairs={{0,48},{16,32},{32,16},{48,0},{1,49},{17,33},{33,17},{49,1},{2,50}... | collective-permute-start | bytes 1572872 | tf_op jit(solution)/shard_map/ppermute | solution.py:288
  87.3 38.1 %collective-permute-start.5 = (f32[512,512]{1,0:T(8,128)}, f32[512,512]{1,0:T(8,128)}, u32[]{:S(2)}, u32[]{:S(2)}) collective-permute-start(f32[512,512]{1,0:T(8,128)} %bitcast.7.c0), channel_id=1, source_target_pairs={{0,16},{16,0},{32,48},{48,32},{1,17},{17,1},{33,49},{49,33},{2,18}... | collective-permute-start | bytes 3145736 | tf_op jit(solution)/shard_map/ppermute | solution.py:288
  88.0 48.1 %collective-permute-start.6 = (f32[512,512]{1,0:T(8,128)}, f32[512,512]{1,0:T(8,128)}, u32[]{:S(2)}, u32[]{:S(2)}) collective-permute-start(f32[512,512]{1,0:T(8,128)} %bitcast.7.c0), channel_id=1, source_target_pairs={{0,32},{16,48},{32,0},{48,16},{1,33},{17,49},{33,1},{49,17},{2,34}... | collective-permute-start | bytes 3145736 | tf_op jit(solution)/shard_map/ppermute | solution.py:288
  89.2 48.3 %collective-permute-start.7 = (f32[512,512]{1,0:T(8,128)}, f32[512,512]{1,0:T(8,128)}, u32[]{:S(2)}, u32[]{:S(2)}) collective-permute-start(f32[512,512]{1,0:T(8,128)} %bitcast.7.c0), channel_id=1, source_target_pairs={{0,48},{16,32},{32,16},{48,0},{1,49},{17,33},{33,17},{49,1},{2,50}... | collective-permute-start | bytes 3145736 | tf_op jit(solution)/shard_map/ppermute | solution.py:288
  92.9 32.0 %all-to-all-start.2 = ((f32[16,32,256]{2,1,0:T(8,128)}), f32[16,32,256]{2,1,0:T(8,128)S(1)}, u32[]{:S(2)}, u32[]{:S(2)}) async-start(f32[16,32,256]{2,1,0:T(8,128)} %broadcast_in_dim.28), calls=%async_computation.2 | async-start | bytes 1048576 | tf_op jit(solution)/shard_map/all_to_all | solution.py:298
  124.0 1.0 copy-start
  125.0 34.2 %collective-permute-start.10 = (f32[512,256]{1,0:T(8,128)S(1)}, f32[512,256]{1,0:T(8,128)S(1)}, u32[]{:S(2)}, u32[]{:S(2)}) collective-permute-start(f32[512,256]{1,0:T(8,128)S(1)} %bitcast.50), channel_id=1, source_target_pairs={{0,48},{16,32},{32,16},{48,0},{1,49},{17,33},{33,17},{49,1},{2,50}... | collective-permute-start | bytes 1572872 | tf_op jit(solution)/shard_map/ppermute | solution.py:288
  125.4 33.8 %collective-permute-start.8 = (f32[512,256]{1,0:T(8,128)S(1)}, f32[512,256]{1,0:T(8,128)S(1)}, u32[]{:S(2)}, u32[]{:S(2)}) collective-permute-start(f32[512,256]{1,0:T(8,128)S(1)} %bitcast.51), channel_id=1, source_target_pairs={{0,16},{16,0},{32,48},{48,32},{1,17},{17,1},{33,49},{49,33},{2,18}... | collective-permute-start | bytes 1572872 | tf_op jit(solution)/shard_map/ppermute | solution.py:288
  125.4 33.8 %collective-permute-start.9 = (f32[512,256]{1,0:T(8,128)S(1)}, f32[512,256]{1,0:T(8,128)S(1)}, u32[]{:S(2)}, u32[]{:S(2)}) collective-permute-start(f32[512,256]{1,0:T(8,128)S(1)} %bitcast.52), channel_id=1, source_target_pairs={{0,32},{16,48},{32,0},{48,16},{1,33},{17,49},{33,1},{49,17},{2,34}... | collective-permute-start | bytes 1572872 | tf_op jit(solution)/shard_map/ppermute | solution.py:288
  159.2 42.5 %copy-start.1 = (f32[512,1024]{1,0:T(8,128)S(1)}, f32[512,1024]{1,0:T(8,128)}, u32[]{:S(2)}) copy-start(f32[512,1024]{1,0:T(8,128)} %get-tuple-element.35) | copy-start | bytes 6291460
Sparse Core Ops, SparseCore 0:
  12.6 26.8 all-gather.2
  43.2 109.2 all-gather.4
